TPU v7x, 32 devices: a whole 2x2x4 slice. The times are simulated.
32 devices in a mesh: sta: 8 (over z, y), tm: 4 (over x, core).
Axes of the slice: x: 2, y: 2, z: 4, core: 2. Of those that a mesh axis runs over, the one named last changes fastest.
Arguments:
- signal: bfloat16 [256, 12288], P('sta', 'tm'), may hold values from -6 to 6
- fir: float32 [4, 32], replicated, may hold values from -1 to 1
- taps: int32 [4], replicated, may hold values from 16 to 32, as said below
- sources: int32 [2, 16], replicated, may hold values from 0 to 255, as said below
Outputs:
- correlations: bfloat16 [2, 4, 16, 256, 512], P(None, None, None, 'sta', 'tm')
Inputs may be any that keep to these rules, and one draw needn't show every extreme that they name: Each band has between 16 and 32 taps, and some band has exactly 32. `sources`: the source channels of one round are distinct.
All inputs are finite; a program needn't handle non-finite values.
Results may differ from a plain program's by a relative error of at most 0.0058.
Values may be sent and summed in bfloat16 or wider, within the bound.
A program may use at most 128 MiB of HBM per device.

v0:
```python
import jax
import jax.numpy as jnp
from jax import lax
from jax.sharding import PartitionSpec as P

ROUNDS = 2
MAXLAG = 256


def passed_along(value, axis, steps):
    count = lax.axis_size(axis)
    first, last = (max(0, -steps), min(count, count - steps))
    return lax.ppermute(value, axis, [(source, source + steps) for source in range(first, last)])


def padded_2(block, sides, width):
    for axis, dim in sides:
        count = lax.axis_size(axis)
        forward = [(i, i + 1) for i in range(count - 1)]
        backward = [(target, source) for source, target in forward]
        low = lax.ppermute(
            lax.slice_in_dim(block, block.shape[dim] - width, None, axis=dim), axis, forward
        )
        high = lax.ppermute(lax.slice_in_dim(block, 0, width, axis=dim), axis, backward)
        block = jnp.concatenate([low, block, high], axis=dim)
    return block


def skew(values, count_rows):
    leading = values.shape[:-1]
    length = values.shape[-1]
    row_width = length + count_rows
    padded = jnp.concatenate([values, jnp.zeros(leading + (count_rows,), values.dtype)], axis=-1)
    repeated = jnp.tile(padded, (1,) * len(leading) + (count_rows,))
    return repeated[..., : count_rows * (row_width - 1)].reshape(
        leading + (count_rows, row_width - 1)
    )


def band_matrix(fir, taps, count_rows):
    tap_limit = fir.shape[1]
    active = jnp.arange(tap_limit, dtype=jnp.int32)[None, :] < taps[:, None]
    coefficients = jnp.where(active, fir, 0.0).astype(jnp.bfloat16)
    return skew(coefficients[:, ::-1], count_rows)


def filter_blocks(extended, fir, taps, length, block):
    tap_limit = fir.shape[1]
    channels = extended.shape[0]
    count = length // block
    main = extended[:, tap_limit - 1 :].reshape(channels, count, block)
    prefix = extended[:, :length].reshape(channels, count, block)[:, :, : tap_limit - 1]
    pieces = jnp.concatenate([prefix, main], axis=2)
    result = jnp.einsum(
        "cnu,btu->bcnt", pieces, band_matrix(fir, taps, block), preferred_element_type=jnp.float32
    )
    return result.reshape(result.shape[0], channels, length)


def correlate(traces, window, lag_count, time_block, lag_block):
    bands = traces.shape[0]
    count_src = traces.shape[1]
    length = traces.shape[2]
    channels = window.shape[1]
    turns = length // time_block
    groups = lag_count // lag_block
    span = time_block + lag_block - 1

    def step(turn, total):
        begin = turn * time_block
        block = lax.dynamic_slice_in_dim(traces, begin, time_block, 2)
        slab = lax.dynamic_slice_in_dim(window, begin, lag_count + time_block - 1, 2)
        parts = []
        for band in range(bands):
            skewed = skew(block[band], lag_block)
            slabs = jnp.stack(
                [slab[band, :, g * lag_block : g * lag_block + span] for g in range(groups)], axis=1
            )
            term = jnp.einsum("sqj,cgj->gqsc", skewed, slabs, preferred_element_type=jnp.float32)
            parts.append(term.reshape(lag_count, count_src, channels))
        return total + jnp.stack(parts, axis=1)

    empty = jnp.zeros((lag_count, bands, count_src, channels), jnp.float32)
    return lax.fori_loop(0, turns, step, empty)


def per_device(signal, fir, taps, sources):
    channels = signal.shape[0]
    samples = signal.shape[1]
    tap_limit = fir.shape[1]
    shards = lax.axis_size("tm")
    samples_all = samples * shards
    lag_count = 2 * MAXLAG
    norm_scale = samples_all ** (-0.5)
    fir_block = min(256, samples)
    widened = None
    left_rim = passed_along(signal[:, samples - (tap_limit - 1) :], "tm", 1)
    extended = jnp.concatenate([left_rim, signal], axis=1)
    filtered = filter_blocks(extended, fir, taps, samples, fir_block).astype(jnp.bfloat16)
    local_ids = sources - lax.axis_index("sta") * channels
    onehot = (local_ids[:, :, None] == jnp.arange(channels, dtype=jnp.int32)[None, None, :]).astype(
        jnp.bfloat16
    )
    results = []
    widened = padded_2(filtered, (("tm", 2),), MAXLAG)
    share = lag_count // shards
    lag_block = min(128, share)
    time_block = min(512, samples)
    for rnd in range(ROUNDS):
        traces = lax.psum(
            jnp.einsum(
                "sc,bct->bst", onehot[rnd], filtered, preferred_element_type=jnp.float32
            ).astype(jnp.bfloat16),
            "sta",
        )

        def lag_terms(start, count, traces=traces):
            return correlate(traces, widened, count, time_block, lag_block) * norm_scale

        summed = lax.psum_scatter(
            lag_terms(jnp.int32(0), share * lax.axis_size("tm")),
            "tm",
            scatter_dimension=0,
            tiled=True,
        ).astype(jnp.bfloat16)
        results.append(jnp.transpose(summed, (1, 2, 3, 0)))
    return jnp.stack(results, axis=0)


def solution(mesh):
    in_specs = (P("sta", "tm"), P(), P(), P())
    out_specs = P(None, None, None, "sta", "tm")
    return jax.shard_map(
        per_device, mesh=mesh, in_specs=in_specs, out_specs=out_specs, check_vma=False
    )
```

profile of v0, /device:TPU:0, one launch (start us, length us, event | category | flops | bytes accessed | tf_op | source)
XLA Modules:
  0.0 960.0 jit_solution(14836553255949783289)
XLA Ops:
  25.8 69.2 %all-reduce.12.cloned.1.call-done = (bf16[4,16,3072]{2,1,0:T(8,128)(2,1)}, bf16[4,16,3072]{2,1,0:T(8,128)(2,1)}) async-done(((bf16[4,16,3072]{2,1,0:T(8,128)(2,1)}, bf16[4,16,3072]{2,1,0:T(8,128)(2,1)}), (bf16[4,16,3072]{2,1,0:T(8,128)(2,1)}, bf16[4,16,3072]{2,1,0:T(8,128)(2,1)})) %all-reduce.12.cloned.1.call-update) | async-done | bytes 786448 | tf_op jit(solution)/shard_map/psum | solution.py:110
  95.0 390.8 %while.28 = (s32[]{:T(128)}, f32[512,4,16,32]{0,3,2,1:T(8,128)}, bf16[4,32,3584]{2,1,0:T(8,128)(2,1)}, bf16[4,16,3072]{2,1,0:T(8,128)(2,1)}, s32[]{:T(128)}, /*i...) while((s32[]{:T(128)}, f32[512,4,16,32]{0,3,2,1:T(8,128)}, ...), condition=%wide.region_2.3_spmd.clone, body=%wide.region_1.2_spmd.clone.sunk | while | flops 1347940352 | bytes 132265400 | solution.py:84
  101.1 7.2 reshape.228
  114.9 7.2 reshape.230
  128.7 7.2 reshape.232
  192.7 7.2 reshape.232
  244.2 7.2 reshape.230
  258.0 7.2 reshape.232
  271.7 7.2 reshape.226
  309.6 7.2 reshape.230
  323.4 7.2 reshape.232
  337.1 7.2 reshape.226
  361.1 7.2 reshape.228
  374.9 7.2 reshape.230
  388.7 7.2 reshape.232
  402.4 7.2 reshape.226
  426.3 7.2 reshape.228
  440.1 7.2 reshape.230
  453.9 7.2 reshape.232
  467.6 7.2 reshape.226
  491.0 411.1 %while.29 = (s32[]{:T(128)}, f32[512,4,16,32]{0,3,2,1:T(8,128)}, bf16[4,32,3584]{2,1,0:T(8,128)(2,1)}, bf16[4,16,3072]{2,1,0:T(8,128)(2,1)}, s32[]{:T(128)}, /*i...) while((s32[]{:T(128)}, f32[512,4,16,32]{0,3,2,1:T(8,128)}, ...), condition=%wide.region_6.7_spmd.clone, body=%wide.region_5.6_spmd.clone.sunk | while | flops 1347940352 | bytes 132265400 | solution.py:84
  530.1 7.2 reshape.238
  543.9 7.2 reshape.240
  908.5 42.4 %reduce-scatter.5.cloned.1.call-done = f32[128,4,16,32]{0,3,2,1:T(8,128)} async-done(((f32[512,4,16,32]{0,3,2,1:T(8,128)}), f32[128,4,16,32]{0,3,2,1:T(8,128)}) %reduce-scatter.5.cloned.1.call-update) | async-done | bytes 1048592 | tf_op jit(solution)/shard_map/reduce_scatter | solution.py:120
  (517 shorter events, 669.1 us)
Async XLA Ops:
  6.5 7.7 copy-start.6
  6.5 88.4 %all-reduce.12.cloned.1.call-start = ((), (), s32[]{:S(2)}) async-start(), calls=%async_computation.4 | async-start | bytes 1572864 | tf_op jit(solution)/shard_map/psum | solution.py:110
  7.4 6.9 collective-permute-start
  17.4 889.8 %reduce-scatter.3.cloned.1.call-start = ((), (), s32[]{:S(2)}) async-start(), calls=%async_computation.2 | async-start | bytes 5242880 | tf_op jit(solution)/shard_map/reduce_scatter | solution.py:120
  17.5 5.8 collective-permute-start.1
  22.0 3.1 collective-permute-start.2
  490.9 460.0 %reduce-scatter.5.cloned.1.call-start = ((), (), s32[]{:S(2)}) async-start(), calls=%async_computation.3 | async-start | bytes 5242880 | tf_op jit(solution)/shard_map/reduce_scatter | solution.py:120
  565.9 4.4 copy-start.1
  565.9 4.4 copy-start.3
  566.0 4.4 copy-start.5
  630.1 4.4 copy-start.1
  630.1 4.4 copy-start.3
  630.1 4.4 copy-start.5
  695.6 4.4 copy-start.1
  695.6 4.4 copy-start.3
  695.6 4.4 copy-start.5
  761.2 4.4 copy-start.1
  761.2 4.4 copy-start.3
  761.2 4.4 copy-start.5
  826.7 4.4 copy-start.1
  826.7 4.4 copy-start.3
  892.0 4.4 copy-start.1
  892.0 4.4 copy-start.3
  892.1 4.4 copy-start.5
  (19 other events, 82.1 us)
Sparse Core Ops, SparseCore 0:
  17.5 77.4 all-reduce.11
  491.0 43.4 reduce-scatter.2
  907.3 43.5 reduce-scatter.4
where the time goes:
time: 968 us; the launch traced here: 960 us
  local copies, waits for them, and re-layouts  675 us (70%)
  waiting for transfers between devices  112 us (12%)
  other arithmetic  80.2 us (8%)
  matrix products  50 us (5%)
  loops' own time  21.3 us (2%)
  between operations  13.5 us (1%)
    reshape x49, local copies, waits for them, and re-layouts, skew(): repeated[..., :count_rows * (row_width - 1)]  349 us
    slice x49, local copies, waits for them, and re-layouts, skew(): repeated[..., :count_rows * (row_width - 1)]  82.5 us
    reshape x48, local copies, waits for them, and re-layouts, step(): return total + jnp.stack(parts, axis=1)  82.2 us
    while x120, local copies, waits for them, and re-layouts  72.3 us
    psum x1, waiting for transfers between devices, per_device(): lax.psum(jnp.einsum('sc,bct->bst', onehot[rnd], filtered, preferred_eleme...  69.2 us
    add x12, other arithmetic, step(): return total + jnp.stack(parts, axis=1)  64.7 us
    dot_general x48, matrix products, step(): jnp.einsum('sqj,cgj->gqsc', skewed, slabs, preferred_element_type=jnp.flo...  47.4 us
    transpose x48, local copies, waits for them, and re-layouts, step(): jnp.einsum('sqj,cgj->gqsc', skewed, slabs, preferred_element_type=jnp.flo...  45.6 us
  transfers between devices with their start and end apart: 6, of which 3 were waited for; matrix products, arithmetic and copies ran while one was open for 42% of the time, Pallas kernels for 0%

commit v1 on v0

v1 whole, which is shorter than its diff:
```python
import functools

import jax
import jax.numpy as jnp
from jax import lax
from jax.experimental import pallas as pl
from jax.experimental.pallas import tpu as pltpu
from jax.sharding import PartitionSpec as P

ROUNDS = 2
MAXLAG = 256
LANES = 128
TILES = 8
CHUNK = 1792


def kernel(
    bands, sources, share, norm_scale,
    own_ref, src_ref, coef_ref, out_ref, raw, own_f, src_f, total,
):
    shards, channels, length = own_ref.shape
    samples = shards * length
    pad = own_f.shape[2] - samples - MAXLAG
    src_pad = src_f.shape[2] - samples - LANES
    rows = channels + sources

    raw[:, :LANES] = jnp.zeros((rows, LANES), raw.dtype)
    for shard in range(shards):
        at = pl.ds(LANES + shard * length, length)
        raw[:channels, at] = own_ref[shard]
        raw[channels:, at] = src_ref[shard]
    for band in range(bands):
        own_f[band, :, :MAXLAG] = jnp.zeros((channels, MAXLAG), own_f.dtype)
        own_f[band, :, pl.ds(MAXLAG + samples, pad)] = jnp.zeros((channels, pad), own_f.dtype)
        src_f[band, :, :LANES] = jnp.zeros((sources, LANES), src_f.dtype)
        src_f[band, :, pl.ds(LANES + samples, src_pad)] = jnp.zeros((sources, src_pad), src_f.dtype)

    weights = []
    for band in range(bands):
        base = jnp.broadcast_to(coef_ref[pl.ds(band, 1), :], (2 * LANES, 2 * LANES))
        turned = pltpu.roll(base, LANES, 1, stride=1, stride_axis=0)
        weights.append(turned[:, :LANES].astype(jnp.bfloat16))
    weights = jnp.concatenate(weights, axis=1)

    def filter_step(step, carry):
        begin = pl.multiple_of(step * (TILES * LANES), TILES * LANES)
        window = raw[:, pl.ds(begin, (TILES + 1) * LANES)]
        stacked = jnp.concatenate(
            [window[:, k * LANES : (k + 2) * LANES] for k in range(TILES)], axis=0
        )
        found = jnp.dot(stacked, weights, preferred_element_type=jnp.float32)
        found = found.astype(jnp.bfloat16)
        for k in range(TILES):
            for band in range(bands):
                part = found[k * rows : (k + 1) * rows, band * LANES : (band + 1) * LANES]
                own_f[band, :, pl.ds(MAXLAG + begin + k * LANES, LANES)] = part[:channels]
                src_f[band, :, pl.ds(LANES + begin + k * LANES, LANES)] = part[channels:]
        return carry

    lax.fori_loop(0, samples // (TILES * LANES), filter_step, 0)

    lag_base = lax.axis_index("tm") * share
    low = LANES // sources
    high = 4
    groups = sources // high
    chunks = (samples + LANES + CHUNK - 1) // CHUNK
    lane = lax.broadcasted_iota(jnp.int32, (16, LANES), 1)

    def band_step(band, carry):
        def chunk_step(chunk, carry):
            begin = pl.multiple_of(chunk * CHUNK, CHUNK)
            src_win = src_f[band, :, pl.ds(begin, CHUNK + LANES)]
            own_win = own_f[
                band, :, pl.ds(pl.multiple_of(begin + lag_base, LANES), CHUNK + LANES)
            ]
            left = jnp.concatenate(
                [own_win[:, high * g : high * g + CHUNK] for g in range(groups)], axis=0
            )
            right = []
            for q_high in range(high):
                for q_low in range(low):
                    shift = LANES - (sources * q_low + q_high)
                    right.append(src_win[:, shift : shift + CHUNK])
            right = jnp.concatenate(right, axis=0)
            term = lax.dot_general(
                left, right, (((1,), (1,)), ((), ())), preferred_element_type=jnp.float32
            )

            @pl.when(chunk == 0)
            def _():
                total[...] = term

            @pl.when(chunk > 0)
            def _():
                total[...] += term

            return carry

        lax.fori_loop(0, chunks, chunk_step, 0)

        for c in range(0, channels, 16):
            blocks = [
                total[g * channels + c : g * channels + c + 16, k * LANES : (k + 1) * LANES]
                for g in range(groups)
                for k in range(high)
            ]
            bit = 1
            while bit < sources:
                odd = (lane & bit) != 0
                for e in range(sources):
                    if e & bit == 0:
                        a, b = blocks[e], blocks[e | bit]
                        blocks[e] = jnp.where(odd, pltpu.roll(b, bit, 1), a)
                        blocks[e | bit] = jnp.where(odd, b, pltpu.roll(a, LANES - bit, 1))
                bit *= 2
            per_round = sources // ROUNDS
            for s in range(sources):
                out_ref[s // per_round, band, s % per_round, c : c + 16, :] = (
                    blocks[s] * norm_scale
                ).astype(out_ref.dtype)
        return carry

    lax.fori_loop(0, bands, band_step, 0)


def per_device(signal, fir, taps, sources):
    channels, length = signal.shape
    bands, tap_limit = fir.shape
    shards = lax.axis_size("tm")
    samples = length * shards
    share = 2 * MAXLAG // shards
    count = sources.size

    active = jnp.arange(tap_limit, dtype=jnp.int32)[None, :] < taps[:, None]
    coefficients = jnp.where(active, fir, 0.0).astype(jnp.bfloat16).astype(jnp.float32)
    coefficients = jnp.pad(coefficients, ((0, 0), (0, 2 * LANES - tap_limit)))

    local_ids = sources.reshape(-1) - lax.axis_index("sta") * channels
    onehot = (local_ids[:, None] == jnp.arange(channels, dtype=jnp.int32)[None, :]).astype(
        jnp.bfloat16
    )
    picked = jnp.dot(onehot, signal, preferred_element_type=jnp.float32).astype(jnp.bfloat16)
    picked = lax.psum(picked, "sta")
    own = lax.all_gather(signal, "tm")
    src = lax.all_gather(picked, "tm")

    chunks = (samples + LANES + CHUNK - 1) // CHUNK
    span = chunks * CHUNK
    return pl.pallas_call(
        functools.partial(kernel, bands, count, share, samples ** (-0.5)),
        out_shape=jax.ShapeDtypeStruct(
            (ROUNDS, bands, count // ROUNDS, channels, share), jnp.bfloat16
        ),
        in_specs=[pl.BlockSpec(memory_space=pltpu.VMEM)] * 3,
        out_specs=pl.BlockSpec(memory_space=pltpu.VMEM),
        scratch_shapes=[
            pltpu.VMEM((channels + count, LANES + samples), jnp.bfloat16),
            pltpu.VMEM((bands, channels, span + LANES + 2 * MAXLAG - share), jnp.bfloat16),
            pltpu.VMEM((bands, count, span + LANES), jnp.bfloat16),
            pltpu.VMEM((count // 4 * channels, 4 * LANES), jnp.float32),
        ],
        compiler_params=pltpu.CompilerParams(vmem_limit_bytes=52 * 2**20),
    )(own, src, coefficients)


def solution(mesh):
    in_specs = (P("sta", "tm"), P(), P(), P())
    out_specs = P(None, None, None, "sta", "tm")
    return jax.shard_map(
        per_device, mesh=mesh, in_specs=in_specs, out_specs=out_specs, check_vma=False
    )
```

time: 968 us -> 135 us (0.14)
  local copies, waits for them, and re-layouts: 675 us -> 1.67 us
  other arithmetic: 80.2 us -> 0.08 us
  waiting for transfers between devices: 112 us -> 63.1 us
  matrix products: 50 us -> 1.86 us
  Pallas kernels: 0 us -> 36.1 us
  loops' own time: 21.3 us -> 0 us
  blocking collectives: 0 us -> 18.9 us
    reshape x99 -> x0, local copies, waits for them, and re-layouts: 431 us -> none  [the longest x49 349 us: skew(): repeated[..., :count_rows * (row_width - 1)]]
    slice x52 -> x0, local copies, waits for them, and re-layouts: 83.4 us -> none  [the longest x49 82.5 us: skew(): repeated[..., :count_rows * (row_width - 1)]]
    while x120 -> x0, local copies, waits for them, and re-layouts: 72.3 us -> none
    add x12 -> x0, other arithmetic: 64.7 us -> none  [step(): return total + jnp.stack(parts, axis=1)]
    dot_general x51 -> x1, matrix products: 50 us -> 1.86 us  [per_device(): jnp.dot(onehot, signal, preferred_element_type=jnp.float32)]
    transpose x48 -> x0, local copies, waits for them, and re-layouts: 45.6 us -> none  [step(): jnp.einsum('sqj,cgj->gqsc', skewed, slabs, preferred_element_type=jnp.flo...]
    reduce_scatter x2 -> x0, waiting for transfers between devices: 42.4 us -> none  [per_device(): lax.psum_scatter(lag_terms(jnp.int32(0), share * lax.axis_size('tm')), 't...]
    pallas_call x0 -> x1, Pallas kernels: none -> 36.1 us  [per_device(): pl.pallas_call(functools.partial(kernel, bands, count, share, samples **...]
  transfers between devices with their start and end apart: 6 -> 1, of which waited for: 3 -> 1; matrix products, arithmetic and copies ran while one was open for 42% -> 0% of each run, Pallas kernels for 0% -> 0%
where the time goes in v1:
time: 135 us
  waiting for transfers between devices  63.1 us (47%)
  Pallas kernels  36.1 us (27%)
  blocking collectives  18.9 us (14%)
  between operations  13.4 us (10%)
  matrix products  1.86 us (1%)
  local copies, waits for them, and re-layouts  1.67 us (1%)
    psum x1, waiting for transfers between devices, per_device(): picked = lax.psum(picked, 'sta')  63.1 us
    pallas_call x1, Pallas kernels, per_device(): pl.pallas_call(functools.partial(kernel, bands, count, share, samples **...  36.1 us
    all_gather x1, blocking collectives, per_device(): own = lax.all_gather(signal, 'tm')  10.2 us
    all_gather x1, blocking collectives, per_device(): src = lax.all_gather(picked, 'tm')  8.77 us
  transfers between devices with their start and end apart: 1, of which 1 were waited for; matrix products, arithmetic and copies ran while one was open for 0% of the time, Pallas kernels for 0%

profile of v1, /device:TPU:0, one launch (start us, length us, event | category | flops | bytes accessed | tf_op | source)
XLA Modules:
  0.0 135.2 jit_solution(18068620500466048841)
XLA Ops:
  6.5 0.0 all-reduce.3.cloned.1.call-start
  6.5 0.0 copy-start.2
  6.5 0.7 copy-done.2
  7.2 0.1 sub.15
  7.3 1.9 %fusion = bf16[1,32,3072]{2,1,0:T(8,128)(2,1)} fusion(bf16[32,3072]{1,0:T(8,128)(2,1)} %param.4, s32[32]{0:T(128)S(1)} %sub.15), kind=kOutput, calls=%fused_computation.1 | convolution fusion | flops 6390784 | bytes 393344 | tf_op jit(solution)/shard_map/dot_general | solution.py:142
  9.2 0.0 copy-start
  9.2 0.0 all-reduce.3.cloned.1.call-update
  9.2 0.9 copy-done
  10.1 0.0 copy-start.1
  10.1 0.0 copy-start.3
  10.1 10.2 %all-gather = bf16[128,3072]{1,0:T(8,128)(2,1)S(1)} all-gather(bf16[32,3072]{1,0:T(8,128)(2,1)S(1)} %copy-done), channel_id=2, replica_groups=mesh['sta'=8,'tm'=4] {'tm'}, dimensions={0}, use_global_device_ids=true | all-gather | bytes 983040 | tf_op jit(solution)/shard_map/all_gather | solution.py:144
  20.3 0.0 copy-done.1
  20.3 0.0 copy-done.3
  20.3 0.1 select_convert_fusion
  20.3 63.1 %all-reduce.3.cloned.1.call-done = bf16[1,32,3072]{2,1,0:T(8,128)(2,1)} async-done(((bf16[1,32,3072]{2,1,0:T(8,128)(2,1)}), bf16[1,32,3072]{2,1,0:T(8,128)(2,1)}) %all-reduce.3.cloned.1.call-update) | async-done | bytes 196624 | tf_op jit(solution)/shard_map/psum | solution.py:143
  83.4 8.8 %all_gather.15.src_ref = bf16[4,32,3072]{2,1,0:T(8,128)(2,1)S(1)} all-gather(bf16[1,32,3072]{2,1,0:T(8,128)(2,1)} %all-reduce.3.cloned.1.call-done), channel_id=1, replica_groups=mesh['sta'=8,'tm'=4] {'tm'}, dimensions={0}, use_global_device_ids=true | all-gather | bytes 983040 | tf_op jit(solution)/shard_map/all_gather | solution.py:145
  92.2 36.1 %shard_map.46 = bf16[2,4,16,32,128]{4,3,2,1,0:T(8,128)(2,1)} custom-call(bf16[4,32,3072]{2,1,0:T(8,128)(2,1)S(1)} %bitcast.4, bf16[4,32,3072]{2,1,0:T(8,128)(2,1)S(1)} %all_gather.15.src_ref, f32[4,256]{1,0:T(4,128)S(1)} %pad_convert_fusion.coef_ref), custom_call_target="tpu_custom_call" | custom-call | tf_op jit(solution)/shard_map/pallas_call | solution.py:149
  (2 shorter events, 0.0 us)
Async XLA Ops:
  6.5 76.9 %all-reduce.3.cloned.1.call-start = ((), (), s32[]{:S(2)}) async-start(), calls=%async_computation | async-start | bytes 393216 | tf_op jit(solution)/shard_map/psum | solution.py:143
  6.5 0.7 copy-start.2
  9.2 0.9 copy-start
  10.1 10.2 %copy-start.1 = (f32[4,32]{1,0:T(4,128)S(1)}, f32[4,32]{1,0:T(4,128)}, u32[]{:S(2)}) copy-start(f32[4,32]{1,0:T(4,128)} %param.5) | copy-start | bytes 1540
  10.1 10.2 %copy-start.3 = (s32[4]{0:T(128)S(1)}, s32[4]{0:T(128)}, u32[]{:S(2)}) copy-start(s32[4]{0:T(128)} %param.6) | copy-start | bytes 52
Sparse Core Ops, SparseCore 0:
  10.7 72.7 all-reduce.2

commit v2 on v1

v2 whole, which is shorter than its diff:
```python
import functools

import jax
import jax.numpy as jnp
from jax import lax
from jax.experimental import pallas as pl
from jax.experimental.pallas import tpu as pltpu
from jax.sharding import PartitionSpec as P

ROUNDS = 2
MAXLAG = 256
LANES = 128
TILES = 8
MESH = pl.DeviceIdType.MESH
CHUNK = 1792


def kernel(
    bands, inner, norm_scale,
    signal_ref, ids_ref, coef_ref, out_ref,
    own_raw, src_raw, part, landed, across, raw, own_f, src_f, shifted, total,
    rs_send, rs_recv, out_send, out_recv, ag_send, ag_recv, x_send, x_recv,
    core_send, core_recv, own_send, own_recv,
):
    shards, channels, length = own_raw.shape
    sources = ids_ref.shape[0]
    outer = lax.axis_size("sta") // inner
    piece = length // inner
    samples = shards * length
    share = 2 * MAXLAG // shards
    pad = own_f.shape[2] - samples - MAXLAG
    src_pad = src_f.shape[2] - samples - LANES
    span = shifted.shape[2]

    sta, tm = lax.axis_index("sta"), lax.axis_index("tm")
    base, mine = (sta // inner) * inner, sta % inner
    far = (tm + shards // 2) % shards
    twin = tm + 1 - 2 * (tm % 2)
    far_twin = (twin + shards // 2) % shards

    def near(k):
        return base + (mine + k + inner) % inner

    def group(k):
        return (sta + k * inner + outer * inner) % (outer * inner)

    def send(src, dst, send_sem, recv_sem, device):
        return pltpu.make_async_remote_copy(
            src_ref=src, dst_ref=dst, send_sem=send_sem, recv_sem=recv_sem,
            device_id=device, device_id_type=MESH,
        )

    barrier = pltpu.get_barrier_semaphore()
    partners = [(near(k), tm) for k in range(1, inner)]
    partners += [(group(k), tm) for k in range(1, outer)]
    partners += [(sta, far), (sta, twin)]
    for partner in partners:
        pl.semaphore_signal(barrier, inc=1, device_id=partner, device_id_type=MESH)

    local = ids_ref[...] - sta * channels
    onehot = (
        local == lax.broadcasted_iota(jnp.int32, (sources, channels), 1)
    ).astype(jnp.float32).astype(jnp.bfloat16)
    own_raw[tm] = signal_ref[...]
    for j in range(inner):
        part[j] = jnp.dot(
            onehot, signal_ref[:, j * piece : (j + 1) * piece], preferred_element_type=jnp.float32
        ).astype(jnp.bfloat16)

    pl.semaphore_wait(barrier, len(partners))

    scatter = []
    for k in range(1, inner):
        to = (mine + k) % inner
        copy = send(part.at[to], landed.at[k], rs_send.at[k], rs_recv.at[k], (near(k), tm))
        copy.start()
        scatter.append(copy)
    own_far = send(own_raw.at[tm], own_raw.at[tm], own_send.at[0], own_recv.at[0], (sta, far))
    own_far.start()
    own_twin = send(own_raw.at[tm], own_raw.at[tm], own_send.at[1], own_recv.at[1], (sta, twin))
    own_twin.start()

    raw[:, :LANES] = jnp.zeros((raw.shape[0], LANES), raw.dtype)
    for band in range(bands):
        own_f[band, :, :MAXLAG] = jnp.zeros((channels, MAXLAG), own_f.dtype)
        own_f[band, :, pl.ds(MAXLAG + samples, pad)] = jnp.zeros((channels, pad), own_f.dtype)
        src_f[band, :, :LANES] = jnp.zeros((sources, LANES), src_f.dtype)
        src_f[band, :, pl.ds(LANES + samples, src_pad)] = jnp.zeros((sources, src_pad), src_f.dtype)

    weights = []
    for band in range(bands):
        row = jnp.broadcast_to(coef_ref[pl.ds(band, 1), :], (2 * LANES, 2 * LANES))
        turned = pltpu.roll(row, LANES, 1, stride=1, stride_axis=0)
        weights.append(turned[:, :LANES].astype(jnp.bfloat16))
    weights = jnp.concatenate(weights, axis=1)

    summed = part[mine].astype(jnp.float32)
    for k in range(1, inner):
        scatter[k - 1].wait_recv()
        summed += landed[k].astype(jnp.float32)
    if outer > 1:
        across[0] = summed.astype(jnp.bfloat16)
        exchange = []
        for k in range(1, outer):
            copy = send(
                across.at[0], across.at[k], out_send.at[k], out_recv.at[k], (group(k), tm)
            )
            copy.start()
            exchange.append(copy)
        for copy in exchange:
            copy.wait_recv()
        for k in range(1, outer):
            summed += across[k].astype(jnp.float32)
        for copy in exchange:
            copy.wait_send()
    src_raw[tm, mine] = summed.astype(jnp.bfloat16)

    own_slot = src_raw.at[tm, mine]
    gather = []
    for k in range(1, inner):
        copy = send(own_slot, own_slot, ag_send.at[k], ag_recv.at[k], (near(k), tm))
        copy.start()
        gather.append(copy)
    along = [send(own_slot, own_slot, x_send.at[0], x_recv.at[0], (sta, far))]
    along[0].start()

    own_from_far = send(
        own_raw.at[far], own_raw.at[far], own_send.at[2], own_recv.at[0], (sta, twin)
    )
    own_from_far.wait_recv()
    own_pass = send(own_raw.at[far], own_raw.at[far], own_send.at[2], own_recv.at[2], (sta, twin))
    own_pass.start()

    def arrived(k):
        slot = src_raw.at[tm, (mine - k + inner) % inner]
        send(slot, slot, ag_send.at[k], ag_recv.at[k], (near(k), tm)).wait_recv()
        copy = send(slot, slot, x_send.at[k], x_recv.at[k], (sta, far))
        copy.start()
        along.append(copy)

    for k in range(1, inner):
        arrived(k)
    row_twin = send(src_raw.at[tm], src_raw.at[tm], core_send.at[0], core_recv.at[0], (sta, twin))
    row_twin.start()

    own_twin.wait_recv()
    own_pass.wait_recv()
    for shard in range(shards):
        raw[:channels, pl.ds(LANES + shard * length, length)] = own_raw[shard]

    def filtered(first, rows, target, offset):
        def filter_step(step, carry):
            begin = pl.multiple_of(step * (TILES * LANES), TILES * LANES)
            window = raw[first : first + rows, pl.ds(begin, (TILES + 1) * LANES)]
            stacked = jnp.concatenate(
                [window[:, k * LANES : (k + 2) * LANES] for k in range(TILES)], axis=0
            )
            found = jnp.dot(stacked, weights, preferred_element_type=jnp.float32)
            found = found.astype(jnp.bfloat16)
            for k in range(TILES):
                for band in range(bands):
                    target[band, :, pl.ds(offset + begin + k * LANES, LANES)] = found[
                        k * rows : (k + 1) * rows, band * LANES : (band + 1) * LANES
                    ]
            return carry

        lax.fori_loop(0, samples // (TILES * LANES), filter_step, 0)

    low = LANES // sources
    high = 4
    groups = sources // high
    chunks = span // CHUNK
    lag_base = tm * share

    filtered(0, channels, own_f, MAXLAG)

    for k in range(inner):
        slot = src_raw.at[far, (mine - k + inner) % inner]
        send(slot, slot, x_send.at[k], x_recv.at[k], (sta, far)).wait_recv()
    far_pass = send(src_raw.at[far], src_raw.at[far], core_send.at[1], core_recv.at[1], (sta, twin))
    far_pass.start()

    def shift_band(band, carry):
        def shift_step(chunk, carry):
            begin = pl.multiple_of(chunk * CHUNK, CHUNK)
            window = own_f[
                band, :, pl.ds(pl.multiple_of(begin + lag_base, LANES), CHUNK + LANES)
            ]
            for g in range(groups):
                shifted[band, pl.ds(g * channels, channels), pl.ds(begin, CHUNK)] = window[
                    :, high * g : high * g + CHUNK
                ]
            return carry

        return lax.fori_loop(0, chunks, shift_step, carry)

    lax.fori_loop(0, bands, shift_band, 0)

    for source, index in ((twin, 0), (far_twin, 1)):
        slot = src_raw.at[source]
        send(slot, slot, core_send.at[index], core_recv.at[index], (sta, twin)).wait_recv()
    for shard in range(shards):
        for j in range(inner):
            raw[channels:, pl.ds(LANES + shard * length + j * piece, piece)] = src_raw[shard, j]
    for copy in scatter + gather + along + [own_far, own_twin, own_pass, row_twin, far_pass]:
        copy.wait_send()

    filtered(channels, sources, src_f, LANES)

    lane = lax.broadcasted_iota(jnp.int32, (16, LANES), 1)

    def band_step(band, carry):
        def chunk_step(chunk, carry):
            begin = pl.multiple_of(chunk * CHUNK, CHUNK)
            src_win = src_f[band, :, pl.ds(begin, CHUNK + LANES)]
            left = shifted[band, :, pl.ds(begin, CHUNK)]
            right = []
            for q_high in range(high):
                for q_low in range(low):
                    shift = LANES - (sources * q_low + q_high)
                    right.append(src_win[:, shift : shift + CHUNK])
            right = jnp.concatenate(right, axis=0)
            term = lax.dot_general(
                left, right, (((1,), (1,)), ((), ())), preferred_element_type=jnp.float32
            )

            @pl.when(chunk == 0)
            def _():
                total[...] = term

            @pl.when(chunk > 0)
            def _():
                total[...] += term

            return carry

        lax.fori_loop(0, chunks, chunk_step, 0)

        for c in range(0, channels, 16):
            blocks = [
                total[g * channels + c : g * channels + c + 16, k * LANES : (k + 1) * LANES]
                for g in range(groups)
                for k in range(high)
            ]
            bit = 1
            while bit < sources:
                odd = (lane & bit) != 0
                for e in range(sources):
                    if e & bit == 0:
                        a, b = blocks[e], blocks[e | bit]
                        blocks[e] = jnp.where(odd, pltpu.roll(b, bit, 1), a)
                        blocks[e | bit] = jnp.where(odd, b, pltpu.roll(a, LANES - bit, 1))
                bit *= 2
            per_round = sources // ROUNDS
            for s in range(sources):
                out_ref[s // per_round, band, s % per_round, c : c + 16, :] = (
                    blocks[s] * norm_scale
                ).astype(out_ref.dtype)
        return carry

    lax.fori_loop(0, bands, band_step, 0)


def per_device(signal, fir, taps, sources):
    channels, length = signal.shape
    bands, tap_limit = fir.shape
    shards, stations = lax.axis_size("tm"), lax.axis_size("sta")
    samples = length * shards
    share = 2 * MAXLAG // shards
    count = sources.size
    inner = max(
        d for d in range(1, stations + 1) if stations % d == 0 and length % (d * LANES) == 0
    )
    outer = stations // inner
    piece = length // inner

    active = jnp.arange(tap_limit, dtype=jnp.int32)[None, :] < taps[:, None]
    coefficients = jnp.where(active, fir, 0.0).astype(jnp.bfloat16).astype(jnp.float32)
    coefficients = jnp.pad(coefficients, ((0, 0), (0, 2 * LANES - tap_limit)))

    chunks = (samples + LANES + CHUNK - 1) // CHUNK
    span = chunks * CHUNK
    groups = count // 4
    dma = pltpu.SemaphoreType.DMA
    return pl.pallas_call(
        functools.partial(kernel, bands, inner, samples ** (-0.5)),
        out_shape=jax.ShapeDtypeStruct(
            (ROUNDS, bands, count // ROUNDS, channels, share), jnp.bfloat16
        ),
        in_specs=[pl.BlockSpec(memory_space=pltpu.VMEM)] * 3,
        out_specs=pl.BlockSpec(memory_space=pltpu.VMEM),
        scratch_shapes=[
            pltpu.VMEM((shards, channels, length), jnp.bfloat16),
            pltpu.VMEM((shards, inner, count, piece), jnp.bfloat16),
            pltpu.VMEM((inner, count, piece), jnp.bfloat16),
            pltpu.VMEM((inner, count, piece), jnp.bfloat16),
            pltpu.VMEM((outer, count, piece), jnp.bfloat16),
            pltpu.VMEM((channels + count, LANES + samples), jnp.bfloat16),
            pltpu.VMEM((bands, channels, span + LANES + 2 * MAXLAG - share), jnp.bfloat16),
            pltpu.VMEM((bands, count, span + LANES), jnp.bfloat16),
            pltpu.VMEM((bands, groups * channels, span), jnp.bfloat16),
            pltpu.VMEM((groups * channels, 4 * LANES), jnp.float32),
            dma((inner,)), dma((inner,)), dma((outer,)), dma((outer,)),
            dma((inner,)), dma((inner,)), dma((inner,)), dma((inner,)),
            dma((2,)), dma((2,)), dma((3,)), dma((3,)),
        ],
        compiler_params=pltpu.CompilerParams(
            vmem_limit_bytes=58 * 2**20, collective_id=0, has_side_effects=True
        ),
    )(signal, sources.reshape(count, 1), coefficients)


def solution(mesh):
    in_specs = (P("sta", "tm"), P(), P(), P())
    out_specs = P(None, None, None, "sta", "tm")
    return jax.shard_map(
        per_device, mesh=mesh, in_specs=in_specs, out_specs=out_specs, check_vma=False
    )
```

time: 135 us -> 66.3 us (0.49)
  waiting for transfers between devices: 63.1 us -> 0 us
  Pallas kernels: 36.1 us -> 61.7 us
  blocking collectives: 18.9 us -> 0 us
  between operations: 13.4 us -> 0.01 us
  matrix products: 1.86 us -> 0 us
  local copies, waits for them, and re-layouts: 1.67 us -> 3.05 us
    psum x1 -> x0, waiting for transfers between devices: 63.1 us -> none  [per_device(): picked = lax.psum(picked, 'sta')]
    pallas_call x1, Pallas kernels: 36.1 us -> 61.7 us  [per_device(): pl.pallas_call(functools.partial(kernel, bands, inner, samples ** (-0.5))...]
    all_gather x2 -> x0, blocking collectives: 18.9 us -> none  [the longest x1 10.2 us: per_device(): own = lax.all_gather(signal, 'tm')]
    dot_general x1 -> x0, matrix products: 1.86 us -> none  [per_device(): jnp.dot(onehot, signal, preferred_element_type=jnp.float32)]
  transfers between devices with their start and end apart: 1 -> 0, of which waited for: 1 -> 0; matrix products, arithmetic and copies ran while one was open for 0% -> 0% of each run, Pallas kernels for 0% -> 0%
where the time goes in v2:
time: 66.3 us; the launch traced here: 66.1 us
  Pallas kernels  61.7 us (93%)
  local copies, waits for them, and re-layouts  3.05 us (5%)
  other arithmetic  1.35 us (2%)
    pallas_call x1, Pallas kernels, per_device(): pl.pallas_call(functools.partial(kernel, bands, inner, samples ** (-0.5))...  61.7 us
    unnamed x3, local copies, waits for them, and re-layouts  2.36 us

profile of v2, /device:TPU:0, one launch (start us, length us, event | category | flops | bytes accessed | tf_op | source)
XLA Modules:
  0.0 66.1 jit_solution(11976874391753279210)
XLA Ops:
  0.0 0.8 %select_convert_fusion = bf16[4,32]{1,0:T(4,128)(2,1)S(1)} fusion(f32[4,32]{1,0:T(4,128)} %param.5, s32[4]{0:T(128)} %param.6), kind=kLoop, calls=%fused_computation.1 | loop fusion | flops 256 | bytes 784 | tf_op jit(solution)/shard_map/convert_element_type | solution.py:278
  0.8 0.0 copy-start
  0.8 0.6 pad_convert_fusion.coef_ref
  1.4 0.1 copy-done
  1.4 0.7 %reshape.5.ids_ref = s32[32,1]{1,0:T(8,128)} reshape(s32[2,16]{1,0:T(2,128)S(1)} %copy-done) | data formatting | bytes 256 | tf_op jit(solution)/shard_map/reshape | solution.py:310
  2.1 61.7 %shard_map.46 = bf16[2,4,16,32,128]{4,3,2,1,0:T(8,128)(2,1)} custom-call(bf16[32,3072]{1,0:T(8,128)(2,1)} %signal_ref.1, s32[32,1]{1,0:T(8,128)} %reshape.5.ids_ref, f32[4,256]{1,0:T(4,128)} %pad_convert_fusion.coef_ref), custom_call_target="tpu_custom_call" | custom-call | tf_op jit(solution)/shard_map/pallas_call | solution.py:285
  63.9 2.3 %copy.7 = bf16[2,4,16,32,128]{4,3,2,1,0:T(8,128)(2,1)} copy(bf16[2,4,16,32,128]{4,3,2,1,0:T(8,128)(2,1)} %shard_map.46) | data formatting | bytes 2097152
Async XLA Ops:
  0.8 0.7 %copy-start = (s32[2,16]{1,0:T(2,128)S(1)}, s32[2,16]{1,0:T(2,128)}, u32[]{:S(2)}) copy-start(s32[2,16]{1,0:T(2,128)} %param.7) | copy-start | bytes 388

commit v3 on v2

--- a/solution.py
+++ b/solution.py
@@ -12,7 +12,7 @@
 LANES = 128
 TILES = 8
 MESH = pl.DeviceIdType.MESH
-CHUNK = 1792
+CHUNK = 12544
 
 
 def kernel(
@@ -138,11 +138,6 @@
         copy.start()
         along.append(copy)
 
-    for k in range(1, inner):
-        arrived(k)
-    row_twin = send(src_raw.at[tm], src_raw.at[tm], core_send.at[0], core_recv.at[0], (sta, twin))
-    row_twin.start()
-
     own_twin.wait_recv()
     own_pass.wait_recv()
     for shard in range(shards):
@@ -172,17 +167,10 @@
     chunks = span // CHUNK
     lag_base = tm * share
 
-    filtered(0, channels, own_f, MAXLAG)
-
-    for k in range(inner):
-        slot = src_raw.at[far, (mine - k + inner) % inner]
-        send(slot, slot, x_send.at[k], x_recv.at[k], (sta, far)).wait_recv()
-    far_pass = send(src_raw.at[far], src_raw.at[far], core_send.at[1], core_recv.at[1], (sta, twin))
-    far_pass.start()
 
     def shift_band(band, carry):
         def shift_step(chunk, carry):
-            begin = pl.multiple_of(chunk * CHUNK, CHUNK)
+            begin = pl.multiple_of(chunk * CHUNK, LANES)
             window = own_f[
                 band, :, pl.ds(pl.multiple_of(begin + lag_base, LANES), CHUNK + LANES)
             ]
@@ -194,7 +182,21 @@
 
         return lax.fori_loop(0, chunks, shift_step, carry)
 
-    lax.fori_loop(0, bands, shift_band, 0)
+    filtered(0, channels, own_f, MAXLAG)
+    early = 1
+    lax.fori_loop(0, early, shift_band, 0)
+    for k in range(1, inner):
+        arrived(k)
+    row_twin = send(src_raw.at[tm], src_raw.at[tm], core_send.at[0], core_recv.at[0], (sta, twin))
+    row_twin.start()
+
+    lax.fori_loop(early, bands, shift_band, 0)
+    for k in range(inner):
+        slot = src_raw.at[far, (mine - k + inner) % inner]
+        send(slot, slot, x_send.at[k], x_recv.at[k], (sta, far)).wait_recv()
+    far_pass = send(src_raw.at[far], src_raw.at[far], core_send.at[1], core_recv.at[1], (sta, twin))
+    far_pass.start()
+
 
     for source, index in ((twin, 0), (far_twin, 1)):
         slot = src_raw.at[source]
@@ -211,7 +213,7 @@
 
     def band_step(band, carry):
         def chunk_step(chunk, carry):
-            begin = pl.multiple_of(chunk * CHUNK, CHUNK)
+            begin = pl.multiple_of(chunk * CHUNK, LANES)
             src_win = src_f[band, :, pl.ds(begin, CHUNK + LANES)]
             left = shifted[band, :, pl.ds(begin, CHUNK)]
             right = []

time: 66.3 us -> 51.8 us (0.78)
  Pallas kernels: 61.7 us -> 47.2 us
    pallas_call x1, Pallas kernels: 61.7 us -> 47.2 us  [per_device(): pl.pallas_call(functools.partial(kernel, bands, inner, samples ** (-0.5))...]
where the time goes in v3:
time: 51.8 us; the launch traced here: 51.6 us
  Pallas kernels  47.2 us (91%)
  local copies, waits for them, and re-layouts  3.05 us (6%)
  other arithmetic  1.35 us (3%)
    pallas_call x1, Pallas kernels, per_device(): pl.pallas_call(functools.partial(kernel, bands, inner, samples ** (-0.5))...  47.2 us
    unnamed x3, local copies, waits for them, and re-layouts  2.36 us

profile of v3, /device:TPU:0, one launch (start us, length us, event | category | flops | bytes accessed | tf_op | source)
XLA Modules:
  0.0 51.6 jit_solution(5677987778826227420)
XLA Ops:
  0.0 0.8 %select_convert_fusion = bf16[4,32]{1,0:T(4,128)(2,1)S(1)} fusion(f32[4,32]{1,0:T(4,128)} %param.5, s32[4]{0:T(128)} %param.6), kind=kLoop, calls=%fused_computation.1 | loop fusion | flops 256 | bytes 784 | tf_op jit(solution)/shard_map/convert_element_type | solution.py:280
  0.8 0.0 copy-start
  0.8 0.6 %pad_convert_fusion.coef_ref = f32[4,256]{1,0:T(4,128)} fusion(bf16[4,32]{1,0:T(4,128)(2,1)S(1)} %select_convert_fusion), kind=kLoop, calls=%fused_computation | loop fusion | flops 1024 | bytes 4352 | tf_op jit(solution)/shard_map/jit(_pad)/pad | solution.py:281
  1.4 0.1 copy-done
  1.4 0.7 %reshape.5.ids_ref = s32[32,1]{1,0:T(8,128)} reshape(s32[2,16]{1,0:T(2,128)S(1)} %copy-done) | data formatting | bytes 256 | tf_op jit(solution)/shard_map/reshape | solution.py:312
  2.1 47.2 %shard_map.46 = bf16[2,4,16,32,128]{4,3,2,1,0:T(8,128)(2,1)} custom-call(bf16[32,3072]{1,0:T(8,128)(2,1)} %signal_ref.1, s32[32,1]{1,0:T(8,128)} %reshape.5.ids_ref, f32[4,256]{1,0:T(4,128)} %pad_convert_fusion.coef_ref), custom_call_target="tpu_custom_call" | custom-call | tf_op jit(solution)/shard_map/pallas_call | solution.py:287
  49.3 2.3 %copy.7 = bf16[2,4,16,32,128]{4,3,2,1,0:T(8,128)(2,1)} copy(bf16[2,4,16,32,128]{4,3,2,1,0:T(8,128)(2,1)} %shard_map.46) | data formatting | bytes 2097152
Async XLA Ops:
  0.8 0.7 %copy-start = (s32[2,16]{1,0:T(2,128)S(1)}, s32[2,16]{1,0:T(2,128)}, u32[]{:S(2)}) copy-start(s32[2,16]{1,0:T(2,128)} %param.7) | copy-start | bytes 388

commit v4 on v3

--- a/solution.py
+++ b/solution.py
@@ -17,13 +17,15 @@
 
 def kernel(
     bands, inner, norm_scale,
-    signal_ref, ids_ref, coef_ref, out_ref,
-    own_raw, src_raw, part, landed, across, raw, own_f, src_f, shifted, total,
+    signal_ref, fir_ref, taps_ref, ids_ref, out_ref,
+    own_raw, src_raw, part, landed, across, raw, own_f, src_f, shifted, total, coef_ref,
     rs_send, rs_recv, out_send, out_recv, ag_send, ag_recv, x_send, x_recv,
     core_send, core_recv, own_send, own_recv,
 ):
     shards, channels, length = own_raw.shape
-    sources = ids_ref.shape[0]
+    rounds, per_round = ids_ref.shape
+    sources = rounds * per_round
+    tap_limit = fir_ref.shape[1]
     outer = lax.axis_size("sta") // inner
     piece = length // inner
     samples = shards * length
@@ -57,7 +59,11 @@
     for partner in partners:
         pl.semaphore_signal(barrier, inc=1, device_id=partner, device_id_type=MESH)
 
-    local = ids_ref[...] - sta * channels
+    at_row = lax.broadcasted_iota(jnp.int32, (sources, channels), 0)
+    ids = jnp.zeros((sources, channels), jnp.int32)
+    for s in range(sources):
+        ids = jnp.where(at_row == s, ids_ref[s // per_round, s % per_round], ids)
+    local = ids - sta * channels
     onehot = (
         local == lax.broadcasted_iota(jnp.int32, (sources, channels), 1)
     ).astype(jnp.float32).astype(jnp.bfloat16)
@@ -87,6 +93,12 @@
         src_f[band, :, :LANES] = jnp.zeros((sources, LANES), src_f.dtype)
         src_f[band, :, pl.ds(LANES + samples, src_pad)] = jnp.zeros((sources, src_pad), src_f.dtype)
 
+    coef_ref[...] = jnp.zeros_like(coef_ref)
+    tap = lax.broadcasted_iota(jnp.int32, (1, tap_limit), 1)
+    for band in range(bands):
+        coef_ref[band : band + 1, :tap_limit] = jnp.where(
+            tap < taps_ref[band], fir_ref[band : band + 1, :], 0.0
+        )
     weights = []
     for band in range(bands):
         row = jnp.broadcast_to(coef_ref[pl.ds(band, 1), :], (2 * LANES, 2 * LANES))
@@ -183,7 +195,7 @@
         return lax.fori_loop(0, chunks, shift_step, carry)
 
     filtered(0, channels, own_f, MAXLAG)
-    early = 1
+    early = 0
     lax.fori_loop(0, early, shift_band, 0)
     for k in range(1, inner):
         arrived(k)
@@ -226,13 +238,7 @@
                 left, right, (((1,), (1,)), ((), ())), preferred_element_type=jnp.float32
             )
 
-            @pl.when(chunk == 0)
-            def _():
-                total[...] = term
-
-            @pl.when(chunk > 0)
-            def _():
-                total[...] += term
+            total[...] = term
 
             return carry
 
@@ -253,7 +259,6 @@
                         blocks[e] = jnp.where(odd, pltpu.roll(b, bit, 1), a)
                         blocks[e | bit] = jnp.where(odd, b, pltpu.roll(a, LANES - bit, 1))
                 bit *= 2
-            per_round = sources // ROUNDS
             for s in range(sources):
                 out_ref[s // per_round, band, s % per_round, c : c + 16, :] = (
                     blocks[s] * norm_scale
@@ -265,7 +270,7 @@
 
 def per_device(signal, fir, taps, sources):
     channels, length = signal.shape
-    bands, tap_limit = fir.shape
+    bands = fir.shape[0]
     shards, stations = lax.axis_size("tm"), lax.axis_size("sta")
     samples = length * shards
     share = 2 * MAXLAG // shards
@@ -276,12 +281,9 @@
     outer = stations // inner
     piece = length // inner
 
-    active = jnp.arange(tap_limit, dtype=jnp.int32)[None, :] < taps[:, None]
-    coefficients = jnp.where(active, fir, 0.0).astype(jnp.bfloat16).astype(jnp.float32)
-    coefficients = jnp.pad(coefficients, ((0, 0), (0, 2 * LANES - tap_limit)))
-
     chunks = (samples + LANES + CHUNK - 1) // CHUNK
     span = chunks * CHUNK
+    assert chunks == 1
     groups = count // 4
     dma = pltpu.SemaphoreType.DMA
     return pl.pallas_call(
@@ -289,7 +291,8 @@
         out_shape=jax.ShapeDtypeStruct(
             (ROUNDS, bands, count // ROUNDS, channels, share), jnp.bfloat16
         ),
-        in_specs=[pl.BlockSpec(memory_space=pltpu.VMEM)] * 3,
+        in_specs=[pl.BlockSpec(memory_space=pltpu.VMEM)] * 2
+        + [pl.BlockSpec(memory_space=pltpu.SMEM)] * 2,
         out_specs=pl.BlockSpec(memory_space=pltpu.VMEM),
         scratch_shapes=[
             pltpu.VMEM((shards, channels, length), jnp.bfloat16),
@@ -302,6 +305,7 @@
             pltpu.VMEM((bands, count, span + LANES), jnp.bfloat16),
             pltpu.VMEM((bands, groups * channels, span), jnp.bfloat16),
             pltpu.VMEM((groups * channels, 4 * LANES), jnp.float32),
+            pltpu.VMEM((bands, 2 * LANES), jnp.float32),
             dma((inner,)), dma((inner,)), dma((outer,)), dma((outer,)),
             dma((inner,)), dma((inner,)), dma((inner,)), dma((inner,)),
             dma((2,)), dma((2,)), dma((3,)), dma((3,)),
@@ -309,7 +313,7 @@
         compiler_params=pltpu.CompilerParams(
             vmem_limit_bytes=58 * 2**20, collective_id=0, has_side_effects=True
         ),
-    )(signal, sources.reshape(count, 1), coefficients)
+    )(signal, fir, taps, sources)
 
 
 def solution(mesh):

time: 51.8 us -> 49.3 us (0.952)
  other arithmetic: 1.35 us -> 0 us
  local copies, waits for them, and re-layouts: 3.05 us -> 2.27 us
    convert_element_type x1 -> x0, other arithmetic: 0.75 us -> none  [per_device(): jnp.where(active, fir, 0.0).astype(jnp.bfloat16).astype(jnp.float32)]
    reshape x1 -> x0, local copies, waits for them, and re-layouts: 0.69 us -> none  [per_device(): sources.reshape(count, 1)]
    pad x1 -> x0, other arithmetic: 0.59 us -> none  [per_device(): coefficients = jnp.pad(coefficients, ((0, 0), (0, 2 * LANES - tap_limit)))]
    unnamed x3 -> x1, local copies, waits for them, and re-layouts: 2.36 us -> 2.27 us
where the time goes in v4:
time: 49.3 us; the launch traced here: 49.2 us
  Pallas kernels  46.9 us (95%)
  local copies, waits for them, and re-layouts  2.27 us (5%)
    pallas_call x1, Pallas kernels, per_device(): pl.pallas_call(functools.partial(kernel, bands, inner, samples ** (-0.5))...  46.9 us
    unnamed x1, local copies, waits for them, and re-layouts  2.27 us

profile of v4, /device:TPU:0, one launch (start us, length us, event | category | flops | bytes accessed | tf_op | source)
XLA Modules:
  0.0 49.2 jit_solution(4963976524461862677)
XLA Ops:
  0.0 46.9 %shard_map.46 = bf16[2,4,16,32,128]{4,3,2,1,0:T(8,128)(2,1)} custom-call(bf16[32,3072]{1,0:T(8,128)(2,1)} %signal_ref.1, f32[4,32]{1,0:T(4,128)} %fir_ref.1, s32[4]{0:T(128)} %taps_ref.1, s32[2,16]{1,0:T(2,128)} %ids_ref.1), custom_call_target="tpu_custom_call" | custom-call | tf_op jit(solution)/shard_map/pallas_call | solution.py:289
  46.9 2.3 %copy.6 = bf16[2,4,16,32,128]{4,3,2,1,0:T(8,128)(2,1)} copy(bf16[2,4,16,32,128]{4,3,2,1,0:T(8,128)(2,1)} %shard_map.46) | data formatting | bytes 2097152
